TPU v7x, 32 devices: a whole 2x2x4 slice. The times are simulated.
32 devices in a mesh: groups: 2 (over y), leaf: 4 (over z), sub: 4 (over x, core).
Axes of the slice: x: 2, y: 2, z: 4, core: 2. Of those that a mesh axis runs over, the one named last changes fastest.
Arguments:
- features: bfloat16 [512, 8192], P(('groups', 'leaf'), 'sub'), parts along dimension 0, may hold values from -6 to 6
- occupancy: int32 [512, 256], P(('groups', 'leaf'), 'sub'), parts along dimension 0, may hold values 0 or 1
- offsets: int32 [512, 13], P(('groups', 'leaf')), parts along dimension 0, may hold values from 1 to 64, as said below
- counts: int32 [512], P(('groups', 'leaf')), parts along dimension 0, may hold values from 1 to 13, as said below
- right_side: float32 [512, 256], P(('groups', 'leaf'), 'sub'), parts along dimension 0, may hold values from -3 to 8
Outputs:
- solution_field: float32 [512, 256], P(('groups', 'leaf'), 'sub'), parts along dimension 0
- residual: float32 [512, 256], P(('groups', 'leaf'), 'sub'), parts along dimension 0
There are 2 independent parts, one for each index of `groups`. A program takes and returns all parts, laid end to end along the dimension named above; each array names one. Nothing has to cross between parts.
Inputs may be any that keep to these rules, and one draw needn't show every extreme that they name: `offsets`: every offset is at least 1 and at most 64; some offset equals 64. `counts`: some leaf uses all 13 slots and some leaf uses one.
All inputs are finite; a program needn't handle non-finite values. No bound on the sum of `occupancy` on one device may be relied on, other than what follows from the above.
Results may differ from a plain program's by a relative error of at most 0.0003.
Values may be sent and summed in bfloat16 or wider, within the bound.
A program may use at most 192 MiB of HBM per device.

v0:
```python
import jax
import jax.numpy as jnp
from jax import lax
from jax.sharding import PartitionSpec as P

ITERS = 3


diag_shift = 0.25


def shifted(x, axis, by):
    peers = lax.axis_size(axis)
    pairs = [(i, i + by) for i in range(peers) if 0 <= i + by < peers]
    return lax.ppermute(x, axis, pairs)


def residual_norm(residual):
    return lax.psum(jnp.sum(residual * residual), ("leaf", "sub"))


def body(features, occupancy, offsets, counts, right_side):
    leaf_count = features.shape[0]
    leaf_pos = lax.axis_index("leaf")
    total_leaves = leaf_count * lax.axis_size("leaf")
    vox_share = right_side.shape[1]
    voxels = vox_share * lax.axis_size("sub")
    feat_width = features.shape[1] * lax.axis_size("sub") // voxels
    owned_flat = lax.all_gather(features, "sub", axis=1, tiled=True)
    ahead_flat = shifted(owned_flat, "leaf", -1)
    owned_feat = owned_flat.reshape((leaf_count, feat_width, voxels))
    ahead_feat = ahead_flat.reshape((leaf_count, feat_width, voxels))
    window = jnp.concatenate([owned_feat, ahead_feat], axis=0)
    window_sq = jnp.sum(jnp.square(window.astype(jnp.float32)), axis=1)
    row_start = lax.axis_index("sub") * vox_share
    own_rows = lax.dynamic_slice_in_dim(owned_feat, row_start, vox_share, 2)
    local_sq = lax.dynamic_slice_in_dim(window_sq[:leaf_count], row_start, vox_share, 1)
    anchor = jnp.arange(leaf_count, dtype=jnp.int32)[:, None]
    target = anchor + offsets
    slot_idx = jnp.arange(offsets.shape[1], dtype=jnp.int32)[None, :]
    usable = (slot_idx < counts[:, None]) & (target + leaf_pos * leaf_count < total_leaves)
    target = jnp.where(usable, target, anchor)
    targets = jnp.concatenate([anchor, target], axis=1)
    slot_weight = jnp.concatenate(
        [jnp.ones((leaf_count, 1), jnp.float32), usable.astype(jnp.float32)], axis=1
    )

    def build_leaf(record):
        row_feat, row_sq, chosen, weight_row = record
        columns = window[chosen]
        inner = jnp.einsum("ca,scb->sab", row_feat, columns, preferred_element_type=jnp.float32)
        distance = row_sq[None, :, None] + window_sq[chosen][:, None, :] - 2.0 * inner
        return jnp.exp(-distance / (2.0 * feat_width)) * weight_row[:, None, None]

    kernel = lax.map(build_leaf, (own_rows, local_sq, targets, slot_weight))
    later_slot = (jnp.arange(targets.shape[1], dtype=jnp.int32) > 0).astype(jnp.float32)
    selector = (
        targets[:, :, None] == jnp.arange(2 * leaf_count, dtype=jnp.int32)[None, None, :]
    ).astype(jnp.float32)
    selector = selector * later_slot[None, :, None]

    def mirror_in(column_part):
        spread = jnp.einsum("lsq,lsb->qb", selector, column_part, precision=lax.Precision.HIGHEST)
        shares = lax.psum_scatter(spread, "sub", scatter_dimension=1, tiled=True)
        returned = shifted(shares[leaf_count:], "leaf", 1)
        return shares[:leaf_count] + returned

    row_sums = jnp.sum(kernel, axis=(1, 3))
    diagonal = diag_shift + (row_sums + mirror_in(jnp.sum(kernel, axis=2))) / voxels
    occupied = occupancy.astype(jnp.float32)
    solution_field = jnp.zeros_like(right_side)
    residual = right_side
    direction = right_side
    norm_now = residual_norm(residual)
    for iteration in range(ITERS):
        masked = occupied * direction
        gathered = lax.all_gather(masked, "sub", axis=1, tiled=True)
        ahead_dir = shifted(gathered.astype(jnp.bfloat16), "leaf", -1).astype(gathered.dtype)
        picked = jnp.concatenate([gathered, ahead_dir], axis=0)[targets]
        forward = jnp.einsum("lsab,lsb->la", kernel, picked, precision=lax.Precision.HIGHEST)
        operate_column_part = jnp.einsum(
            "lsab,la->lsb", kernel, masked, precision=lax.Precision.HIGHEST
        )
        image_vec = (
            diagonal * direction + occupied * (forward + mirror_in(operate_column_part)) / voxels
        )
        step_size = norm_now / lax.psum(jnp.sum(direction * image_vec), ("leaf", "sub"))
        solution_field = solution_field + step_size * direction
        residual = residual - step_size * image_vec
        norm_next = residual_norm(residual)
        direction = residual + norm_next / norm_now * direction
        norm_now = norm_next
    return (solution_field, residual)


def solution(mesh):
    in_specs = (
        P(("groups", "leaf"), "sub"),
        P(("groups", "leaf"), "sub"),
        P(("groups", "leaf"), None),
        P(("groups", "leaf")),
        P(("groups", "leaf"), "sub"),
    )
    out_specs = (P(("groups", "leaf"), "sub"), P(("groups", "leaf"), "sub"))
    return jax.shard_map(body, mesh=mesh, in_specs=in_specs, out_specs=out_specs, check_vma=False)
```

profile of v0, /device:TPU:0, one launch (start us, length us, event | category | flops | bytes accessed | tf_op | source)
XLA Modules:
  0.0 838.8 jit_solution(6202227737268780075)
XLA Ops:
  9.6 6.5 all_gather.13
  18.3 10.7 %all-gather.2.cloned.1.call-done = bf16[64,8192]{1,0:T(8,128)(2,1)} async-done(((bf16[64,2048]{1,0:T(8,128)(2,1)}), bf16[64,8192]{1,0:T(8,128)(2,1)}) %all-gather.2.cloned.1.call-update) | async-done | bytes 1048592 | tf_op jit(solution)/shard_map/all_gather | solution.py:29
  37.0 19.4 %collective-permute-done = bf16[64,8192]{1,0:T(8,128)(2,1)S(1)} collective-permute-done((bf16[64,8192]{1,0:T(8,128)(2,1)}, bf16[64,8192]{1,0:T(8,128)(2,1)S(1)}, u32[]{:S(2)}, u32[]{:S(2)}) %collective-permute-start) | collective-permute-done | bytes 1048608 | tf_op jit(solution)/shard_map/ppermute | solution.py:15
  57.8 251.1 %while.10 = (s32[]{:T(128)}, f32[64,14,64,256]{3,2,1,0:T(8,128)}, f32[64,64]{1,0:T(8,128)S(1)}, s32[64,14]{1,0:T(8,128)S(1)}, f32[128,256]{1,0:T(8,128)S(1)}, /*...) while((s32[]{:T(128)}, f32[64,14,64,256]{3,2,1,0:T(8,128)}, ...), condition=%wide.region_4.5_spmd, body=%wide.region_3.4_spmd.sunk | while | flops 16057388 | bytes 1663273 | solution.py:55
  63.5 2.1 fusion.94
  87.1 2.1 fusion.94
  94.9 2.1 fusion.94
  102.8 2.1 fusion.94
  114.5 2.1 fusion.94
  126.3 2.1 fusion.94
  165.5 2.1 fusion.94
  169.5 2.1 fusion.94
  185.2 2.1 fusion.94
  200.9 2.1 fusion.94
  208.8 2.1 fusion.94
  216.7 2.1 fusion.94
  236.3 2.1 fusion.94
  244.1 2.1 fusion.94
  271.6 2.1 fusion.94
  295.1 2.1 fusion.94
  308.9 34.5 %fusion.64 = f32[64,1,14,256]{3,1,2,0:T(1,128)S(1)} fusion(f32[64,14,64,256]{3,2,1,0:T(8,128)} %get-tuple-element.44, f32[64,64,1,1]{1,2,3,0:T(1,128)S(1)} %copy.55), kind=kOutput, calls=%fused_computation.112 | convolution fusion | flops 176160768 | bytes 59654144 | tf_op jit(solution)/shard_map/lsab,la->lsb/dot_general | solution.py:81
  343.4 2.4 convolution_bitcast_fusion.2
  346.1 18.7 %fusion.58 = (f32[64,14,256]{2,1,0:T(8,128)S(1)}, f32[64,64]{1,0:T(8,128)S(1)}) fusion(f32[64,14,64,256]{3,2,1,0:T(8,128)} %get-tuple-element.44), kind=kLoop, calls=%fused_computation.110 | loop fusion | flops 29126656 | bytes 59654144 | tf_op jit(solution)/shard_map/reduce_sum | solution.py:69
  364.8 2.8 convolution_bitcast_fusion.3
  368.2 2.7 gather_fusion.2
  372.8 3.4 collective-permute-start.3
  376.2 10.6 %reduce-scatter.5.cloned.1.call-done = f32[128,64]{0,1:T(8,128)} async-done(((f32[128,256]{0,1:T(8,128)}), f32[128,64]{0,1:T(8,128)}) %reduce-scatter.5.cloned.1.call-update) | async-done | bytes 32784 | tf_op jit(solution)/shard_map/reduce_scatter | solution.py:64
  387.7 3.4 collective-permute-start.1
  391.1 53.6 %fusion.63 = f32[64,1,64,1]{2,1,3,0:T(1,128)S(1)} fusion(f32[64,14,64,256]{3,2,1,0:T(8,128)} %get-tuple-element.44, f32[64,14,256,1]{2,3,1,0:T(1,128)S(1)} %reshape.178), kind=kOutput, calls=%fused_computation.111 | convolution fusion | flops 176160768 | bytes 59654144 | tf_op jit(solution)/shard_map/lsab,lsb->la/dot_general | solution.py:80
  445.5 30.3 %all-reduce.1 = (f32[]{:T(128)}, f32[]{:T(128)}) all-reduce(f32[]{:T(128)} %multiply_reduce_fusion.6, f32[]{:T(128)} %get-tuple-element.89), channel_id=1, replica_groups=mesh['groups'=2,'leaf'=4,'sub'=4] {'leaf','sub'}, use_global_device_ids=true, to_apply=%region_1.2 | all-reduce | flops 2 | bytes 16 | tf_op jit(solution)/shard_map/psum | solution.py:19
  477.7 30.4 %psum.44 = f32[]{:T(128)} all-reduce(f32[]{:T(128)} %multiply_reduce_fusion.4), channel_id=1, replica_groups=mesh['groups'=2,'leaf'=4,'sub'=4] {'leaf','sub'}, use_global_device_ids=true, to_apply=%region_12.13 | all-reduce | flops 1 | bytes 8 | tf_op jit(solution)/shard_map/psum | solution.py:19
  509.5 34.5 %fusion.66 = f32[64,1,14,256]{3,1,2,0:T(1,128)S(1)} fusion(f32[64,14,64,256]{3,2,1,0:T(8,128)} %get-tuple-element.44, f32[64,64,1,1]{1,2,3,0:T(1,128)S(1)} %copy.59), kind=kOutput, calls=%fused_computation.114 | convolution fusion | flops 176160768 | bytes 59654144 | tf_op jit(solution)/shard_map/lsab,la->lsb/dot_general | solution.py:81
  544.0 2.4 convolution_bitcast_fusion.1
  546.5 5.4 all_gather.14
  553.2 4.9 collective-permute-done.4
  558.4 2.7 gather_fusion.3
  564.3 3.9 collective-permute-start.5
  568.2 53.6 %fusion.65 = f32[64,1,64,1]{2,1,3,0:T(1,128)S(1)} fusion(f32[64,14,64,256]{3,2,1,0:T(8,128)} %get-tuple-element.44, f32[64,14,256,1]{2,3,1,0:T(1,128)S(1)} %reshape.180), kind=kOutput, calls=%fused_computation.113 | convolution fusion | flops 176160768 | bytes 59654144 | tf_op jit(solution)/shard_map/lsab,lsb->la/dot_general | solution.py:80
  622.4 30.3 %psum.45 = f32[]{:T(128)} all-reduce(f32[]{:T(128)} %get-tuple-element.85), channel_id=1, replica_groups=mesh['groups'=2,'leaf'=4,'sub'=4] {'leaf','sub'}, use_global_device_ids=true, to_apply=%region_15.16 | all-reduce | flops 1 | bytes 8 | tf_op jit(solution)/shard_map/psum | solution.py:87
  654.7 30.3 %psum.46 = f32[]{:T(128)} all-reduce(f32[]{:T(128)} %get-tuple-element.83), channel_id=1, replica_groups=mesh['groups'=2,'leaf'=4,'sub'=4] {'leaf','sub'}, use_global_device_ids=true, to_apply=%region_17.18 | all-reduce | flops 1 | bytes 8 | tf_op jit(solution)/shard_map/psum | solution.py:19
  686.4 34.5 %fusion.68 = f32[64,1,14,256]{3,1,2,0:T(1,128)S(1)} fusion(f32[64,14,64,256]{3,2,1,0:T(8,128)} %get-tuple-element.44, f32[64,64,1,1]{1,2,3,0:T(1,128)S(1)} %copy.63), kind=kOutput, calls=%fused_computation.116 | convolution fusion | flops 176160768 | bytes 59654144 | tf_op jit(solution)/shard_map/lsab,la->lsb/dot_general | solution.py:81
  720.9 2.4 convolution_bitcast_fusion
  723.3 5.4 all_gather.15
  730.1 4.9 collective-permute-done.6
  735.2 2.7 gather_fusion.4
  741.2 3.6 collective-permute-start.7
  744.8 53.6 %fusion.67 = f32[64,1,64,1]{2,1,3,0:T(1,128)S(1)} fusion(f32[64,14,64,256]{3,2,1,0:T(8,128)} %get-tuple-element.44, f32[64,14,256,1]{2,3,1,0:T(1,128)S(1)} %reshape.182), kind=kOutput, calls=%fused_computation.115 | convolution fusion | flops 176160768 | bytes 59654144 | tf_op jit(solution)/shard_map/lsab,lsb->la/dot_general | solution.py:80
  799.0 30.3 %psum.47 = f32[]{:T(128)} all-reduce(f32[]{:T(128)} %get-tuple-element.79), channel_id=1, replica_groups=mesh['groups'=2,'leaf'=4,'sub'=4] {'leaf','sub'}, use_global_device_ids=true, to_apply=%region_20.21 | all-reduce | flops 1 | bytes 8 | tf_op jit(solution)/shard_map/psum | solution.py:87
  (528 shorter events, 248.7 us)
Async XLA Ops:
  7.2 21.9 %all-gather.2.cloned.1.call-start = ((), (), s32[]{:S(2)}) async-start(), calls=%async_computation.4 | async-start | bytes 1310720 | tf_op jit(solution)/shard_map/all_gather | solution.py:29
  7.9 364.0 %reduce-scatter.7.cloned.1.call-start = ((), (), s32[]{:S(2)}) async-start(), calls=%async_computation.6 | async-start | bytes 163840 | tf_op jit(solution)/shard_map/reduce_scatter | solution.py:64
  16.1 351.8 %collective-permute-start.2 = (bf16[64,256]{0,1:T(8,128)(2,1)S(1)}, bf16[64,256]{0,1:T(8,128)(2,1)S(1)}, u32[]{:S(2)}, u32[]{:S(2)}) collective-permute-start(bf16[64,256]{0,1:T(8,128)(2,1)S(1)} %convert_element_type.36), channel_id=1, source_target_pairs={{4,0},{8,4},{12,8},{5,1},{9,5},{13,9},{6,2},{10,6},{14,10},{7,3},{... | collective-permute-start | bytes 98312 | tf_op jit(solution)/shard_map/ppermute | solution.py:15
  29.0 27.4 %collective-permute-start = (bf16[64,8192]{1,0:T(8,128)(2,1)}, bf16[64,8192]{1,0:T(8,128)(2,1)S(1)}, u32[]{:S(2)}, u32[]{:S(2)}) collective-permute-start(bf16[64,8192]{1,0:T(8,128)(2,1)} %all-gather.2.cloned.1.call-done), channel_id=1, source_target_pairs={{4,0},{8,4},{12,8},{5,1},{9,5},{13,9},{6,2},{10,6},{14,10},{7,3},{... | collective-permute-start | bytes 3145736 | tf_op jit(solution)/shard_map/ppermute | solution.py:15
  56.7 286.7 %copy-start.4 = (f32[14]{0:T(128)S(1)}, f32[14]{0:T(128)}, u32[]{:S(2)}) copy-start(f32[14]{0:T(128)} %compare_convert_fusion) | copy-start | bytes 172
  345.8 41.0 %reduce-scatter.5.cloned.1.call-start = ((), (), s32[]{:S(2)}) async-start(), calls=%async_computation.5 | async-start | bytes 163840 | tf_op jit(solution)/shard_map/reduce_scatter | solution.py:64
  367.6 195.8 %reduce-scatter.9.cloned.1.call-start = ((), (), s32[]{:S(2)}) async-start(), calls=%async_computation.7 | async-start | bytes 163840 | tf_op jit(solution)/shard_map/reduce_scatter | solution.py:64
  371.9 72.9 %copy-start = (f32[128,64]{0,1:T(8,128)S(1)}, f32[128,64]{0,1:T(8,128)}, u32[]{:S(2)}) copy-start(f32[128,64]{0,1:T(8,128)} %reduce-scatter.7.cloned.1.call-done) | copy-start | bytes 98308
  372.8 72.0 %collective-permute-start.3 = (f32[64,64]{0,1:T(8,128)S(1)}, f32[64,64]{0,1:T(8,128)S(1)}, u32[]{:S(2)}, u32[]{:S(2)}) collective-permute-start(f32[64,64]{0,1:T(8,128)S(1)} %slice.50), channel_id=1, source_target_pairs={{0,4},{4,8},{8,12},{1,5},{5,9},{9,13},{2,6},{6,10},{10,14},{3,7},{... | collective-permute-start | bytes 49160 | tf_op jit(solution)/shard_map/ppermute | solution.py:15
  386.8 58.0 %copy-start.1 = (f32[128,64]{0,1:T(8,128)S(1)}, f32[128,64]{0,1:T(8,128)}, u32[]{:S(2)}) copy-start(f32[128,64]{0,1:T(8,128)} %reduce-scatter.5.cloned.1.call-done) | copy-start | bytes 98308
  387.7 57.1 %collective-permute-start.1 = (f32[64,64]{0,1:T(8,128)S(1)}, f32[64,64]{0,1:T(8,128)S(1)}, u32[]{:S(2)}, u32[]{:S(2)}) collective-permute-start(f32[64,64]{0,1:T(8,128)S(1)} %slice.48), channel_id=1, source_target_pairs={{0,4},{4,8},{8,12},{1,5},{5,9},{9,13},{2,6},{6,10},{10,14},{3,7},{... | collective-permute-start | bytes 49160 | tf_op jit(solution)/shard_map/ppermute | solution.py:15
  546.4 193.9 %reduce-scatter.11.cloned.1.call-start = ((), (), s32[]{:S(2)}) async-start(), calls=%async_computation.8 | async-start | bytes 163840 | tf_op jit(solution)/shard_map/reduce_scatter | solution.py:64
  551.9 6.2 collective-permute-start.4
  563.4 58.4 %copy-start.3 = (f32[128,64]{0,1:T(8,128)S(1)}, f32[128,64]{0,1:T(8,128)}, u32[]{:S(2)}) copy-start(f32[128,64]{0,1:T(8,128)} %reduce-scatter.9.cloned.1.call-done) | copy-start | bytes 98308
  564.3 57.5 %collective-permute-start.5 = (f32[64,64]{0,1:T(8,128)S(1)}, f32[64,64]{0,1:T(8,128)S(1)}, u32[]{:S(2)}, u32[]{:S(2)}) collective-permute-start(f32[64,64]{0,1:T(8,128)S(1)} %slice.52), channel_id=1, source_target_pairs={{0,4},{4,8},{8,12},{1,5},{5,9},{9,13},{2,6},{6,10},{10,14},{3,7},{... | collective-permute-start | bytes 49160 | tf_op jit(solution)/shard_map/ppermute | solution.py:15
  728.8 6.2 collective-permute-start.6
  740.3 58.1 %copy-start.2 = (f32[128,64]{0,1:T(8,128)S(1)}, f32[128,64]{0,1:T(8,128)}, u32[]{:S(2)}) copy-start(f32[128,64]{0,1:T(8,128)} %reduce-scatter.11.cloned.1.call-done) | copy-start | bytes 98308
  741.2 57.2 %collective-permute-start.7 = (f32[64,64]{0,1:T(8,128)S(1)}, f32[64,64]{0,1:T(8,128)S(1)}, u32[]{:S(2)}, u32[]{:S(2)}) collective-permute-start(f32[64,64]{0,1:T(8,128)S(1)} %slice.54), channel_id=1, source_target_pairs={{0,4},{4,8},{8,12},{1,5},{5,9},{9,13},{2,6},{6,10},{10,14},{3,7},{... | collective-permute-start | bytes 49160 | tf_op jit(solution)/shard_map/ppermute | solution.py:15
Sparse Core Ops, SparseCore 0:
  9.6 19.4 all-gather.1
  345.9 18.6 reduce-scatter.6
  367.7 19.0 reduce-scatter.4
  546.5 16.8 reduce-scatter.8
  723.4 16.8 reduce-scatter.10
where the time goes:
time: 852 us; the launch traced here: 839 us
  matrix products  406 us (48%)
  blocking collectives  169 us (20%)
  local copies, waits for them, and re-layouts  140 us (16%)
  waiting for transfers between devices  54.1 us (6%)
  other arithmetic  28.2 us (3%)
  between operations  21.2 us (2%)
  starting transfers between devices  19.8 us (2%)
    dot_general x3, matrix products, body(): jnp.einsum('lsab,lsb->la', kernel, picked, precision=lax.Precision.HIGHEST)  161 us
    dot_general x64, matrix products, build_leaf(): jnp.einsum('ca,scb->sab', row_feat, columns, preferred_element_type=jnp.f...  132 us
    dot_general x3, matrix products, body(): jnp.einsum('lsab,la->lsb', kernel, masked, precision=lax.Precision.HIGHEST)  103 us
    psum x3, blocking collectives, residual_norm(): return lax.psum(jnp.sum(residual * residual), ('leaf', 'sub'))  90.9 us
    psum x2, blocking collectives, body(): lax.psum(jnp.sum(direction * image_vec), ('leaf', 'sub'))  60.6 us
    mul x64, local copies, waits for them, and re-layouts, build_leaf(): return jnp.exp(-distance / (2.0 * feat_width)) * weight_row[:, None, None]  44.7 us
    gather x64, local copies, waits for them, and re-layouts, build_leaf(): window_sq[chosen][:, None, :]  36.7 us
    gather x64, local copies, waits for them, and re-layouts, build_leaf(): columns = window[chosen]  35.8 us
  transfers between devices with their start and end apart: 13, of which 7 were waited for; matrix products, arithmetic and copies ran while one was open for 59% of the time, Pallas kernels for 0%

commit v1 on v0

v1 whole, which is shorter than its diff:
```python
import functools

import jax
import jax.numpy as jnp
from jax import lax
from jax.experimental import pallas as pl
from jax.experimental.pallas import tpu as pltpu
from jax.sharding import PartitionSpec as P

ITERS = 3
GROUP = 4
LANES = 128
VMEM_LIMIT = 48 * 1024 * 1024
diag_shift = 0.25
MESH = pl.DeviceIdType.MESH


def shifted(x, axis, by):
    peers = lax.axis_size(axis)
    pairs = [(i, i + by) for i in range(peers) if 0 <= i + by < peers]
    return lax.ppermute(x, axis, pairs)


def apply_kernel(with_ones, rows_at, cols_at, mirror_at, groups_ref, row_ref, col_ref, u_ref, v_ref,
                 fwd_ref, mir_ref, u_wide, fwd_acc, mir_acc):
    leaves, share = u_ref.shape
    voxels = v_ref.shape[1]
    u_wide[...] = jnp.broadcast_to(u_ref[...][:, :, None], u_wide.shape)
    fwd_acc[...] = jnp.zeros_like(fwd_acc)
    mir_acc[...] = jnp.zeros_like(mir_acc)

    def fold_lanes(x):
        return sum(x[:, i:i + LANES] for i in range(0, voxels, LANES))

    def fold_rows(x):
        return sum(x[i:i + 8, :] for i in range(0, share, 8))

    def group(g, carry):
        for i in range(GROUP):
            at = g * GROUP + i
            row = rows_at[at]
            col = cols_at[at]
            mir = mirror_at[at]
            row_read = jnp.minimum(row, leaves - 1)
            block = jnp.exp(
                jnp.dot(row_ref[row_read], col_ref[col], preferred_element_type=jnp.float32)
            )
            v_row = v_ref[pl.ds(col, 1), :]
            wide = u_wide[row_read]
            wide = jnp.concatenate([wide] * (voxels // LANES), axis=1)
            fwd_acc[0, row] += fold_lanes(block * v_row)
            mir_acc[0, mir] += fold_rows(block * wide)
            if with_ones:
                fwd_acc[1, row] += fold_lanes(block)
                mir_acc[1, mir] += fold_rows(block)
        return carry

    lax.fori_loop(0, groups_ref[0], group, 0)
    for n in range(fwd_ref.shape[0]):
        fwd_ref[n] = jnp.sum(fwd_acc[n, :leaves], axis=-1)
        mir_ref[n] = jnp.sum(mir_acc[n, :2 * leaves], axis=1)


def apply_blocks(with_ones, lists, row_feat, col_feat, u, v):
    leaves, share = u.shape
    voxels = v.shape[1]
    count = 2 if with_ones else 1
    smem = pl.BlockSpec(memory_space=pltpu.SMEM)
    vmem = pl.BlockSpec(memory_space=pltpu.VMEM)
    return pl.pallas_call(
        functools.partial(apply_kernel, with_ones),
        out_shape=(
            jax.ShapeDtypeStruct((count, leaves, share), jnp.float32),
            jax.ShapeDtypeStruct((count, 2 * leaves, voxels), jnp.float32),
        ),
        in_specs=[smem] * 4 + [vmem] * 4,
        out_specs=(vmem, vmem),
        scratch_shapes=[
            pltpu.VMEM((leaves, share, LANES), jnp.float32),
            pltpu.VMEM((count, leaves + 1, share, LANES), jnp.float32),
            pltpu.VMEM((count, 2 * leaves + 1, 8, voxels), jnp.float32),
        ],
        compiler_params=pltpu.CompilerParams(vmem_limit_bytes=VMEM_LIMIT),
    )(*lists, row_feat, col_feat, u, v)


def update_kernel(first, last, n_leaf, n_sub, *refs):
    refs = list(refs)
    fwd_ref, mir_ref, occ_ref, dir_ref = refs[:4]
    del refs[:4]
    if first:
        window_ref = refs.pop(0)
        out_refs = refs[:7]
        del refs[:7]
        x_out, res_out, dir_out, u_out, win_dir_out, win_res_out, diag_out = out_refs
    else:
        diag_ref, x_ref, res_ref = refs[:3]
        del refs[:3]
        if last:
            x_out, res_out = refs[:2]
            del refs[:2]
        else:
            win_dir_ref, win_res_ref = refs[:2]
            x_out, res_out, dir_out, u_out, win_dir_out, win_res_out = refs[2:8]
            del refs[:8]
    mir_send, mir_own, mir_back, img_own, img_ahead, scalars, send_sem, recv_sem = refs

    group_at = lax.axis_index("groups")
    leaf_at = lax.axis_index("leaf")
    sub_at = lax.axis_index("sub")
    devices = n_leaf * n_sub
    leaves, share = dir_ref.shape
    voxels = share * n_sub

    def peer(leaf_by, sub_by):
        return (
            group_at,
            lax.rem(leaf_at + leaf_by, n_leaf),
            lax.rem(sub_at + sub_by, n_sub),
        )

    barrier = pltpu.get_barrier_semaphore()

    def greet(k, carry):
        pl.semaphore_signal(barrier, inc=1, device_id=peer(k // n_sub, k % n_sub), device_id_type=MESH)
        return carry

    lax.fori_loop(1, devices, greet, 0)
    for s in range(n_sub):
        mir_send[s] = mir_ref[:, :, s * share:(s + 1) * share]
    pl.semaphore_wait(barrier, devices - 1)

    def copy(src, dst, sem, leaf_by, sub_by):
        return pltpu.make_async_remote_copy(
            src_ref=src, dst_ref=dst, send_sem=send_sem.at[sem], recv_sem=recv_sem.at[sem],
            device_id=peer(leaf_by, sub_by), device_id_type=MESH,
        )

    copies = []
    for s in range(n_sub):
        to = lax.rem(sub_at + s, n_sub)
        copies.append(copy(mir_send.at[to, :, leaves:], mir_back.at[s], s, 1, s))
        copies[-1].start()
    for s in range(1, n_sub):
        to = lax.rem(sub_at + s, n_sub)
        copies.append(copy(mir_send.at[to, :, :leaves], mir_own.at[s], n_sub + s, 0, s))
        copies[-1].start()
    total = fwd_ref[...] + mir_send[sub_at, :, :leaves]
    for c in copies:
        c.wait()
    for s in range(1, n_sub):
        total += mir_own[s]
    for s in range(n_sub):
        total += mir_back[s]
    occ = occ_ref[...]
    direction = dir_ref[...]
    if first:
        diagonal = diag_shift + total[1] / voxels
        residual = direction
        field = jnp.zeros_like(direction)
        diag_out[...] = diagonal
    else:
        diagonal = diag_ref[...]
        residual = res_ref[...]
        field = x_ref[...]
    image = diagonal * direction + occ * total[0] / voxels
    sums = (residual * residual, direction * image, residual * image, image * image)
    sub_iota = lax.broadcasted_iota(jnp.int32, (8, LANES), 0)
    packed = jnp.zeros((8, LANES), jnp.float32)
    for i, term in enumerate(sums):
        packed = jnp.where(sub_iota == i, jnp.sum(term), packed)
    scalars[0] = packed

    def tell(k, carry):
        copy(scalars.at[0], scalars.at[k], 4 * n_sub, k // n_sub, k % n_sub).start()
        return carry

    lax.fori_loop(1, devices, tell, 0)
    copies = []
    if not last:
        img_own[0] = occ * image
        for s in range(n_sub):
            copies.append(copy(img_own.at[0], img_ahead.at[s], 2 * n_sub + s, n_leaf - 1, s))
            copies[-1].start()
        for s in range(1, n_sub):
            copies.append(copy(img_own.at[0], img_own.at[s], 3 * n_sub + s, 0, s))
            copies[-1].start()
    everyone = copy(scalars.at[1:], scalars.at[1:], 4 * n_sub, 1, 0)
    everyone.wait()
    sums = jnp.sum(scalars[...], axis=0)
    rr = sums[0:1, :]
    step = rr / sums[1:2, :]
    new = rr - 2.0 * step * sums[2:3, :] + step * step * sums[3:4, :]
    beta = new / rr
    step_own = step[:, :share]
    beta_own = beta[:, :share]
    x_out[...] = field + step_own * direction
    residual = residual - step_own * image
    res_out[...] = residual
    if last:
        return
    direction = residual + beta_own * direction
    dir_out[...] = direction
    u_out[...] = occ * direction
    for c in copies:
        c.wait()
    if first:
        win_dir_ref = win_res_ref = window_ref
    step_wide = step[:, :1]
    beta_wide = beta[:, :1]
    for part, held in enumerate((img_own, img_ahead)):
        image_window = jnp.concatenate(
            [held[lax.rem(sub_at - s + n_sub, n_sub)] for s in range(n_sub)], axis=1
        )
        rows = slice(part * leaves, (part + 1) * leaves)
        res_window = win_res_ref[rows, :] - step_wide * image_window
        win_res_out[rows, :] = res_window
        win_dir_out[rows, :] = res_window + beta_wide * win_dir_ref[rows, :]


def update(first, last, collective_id, args):
    n_leaf, n_sub = lax.axis_size("leaf"), lax.axis_size("sub")
    count = 2 if first else 1
    leaves, share = args[3].shape
    voxels = share * n_sub
    own = jax.ShapeDtypeStruct((leaves, share), jnp.float32)
    window = jax.ShapeDtypeStruct((2 * leaves, voxels), jnp.float32)
    out_shape = (own, own) if last else (own, own, own, own, window, window)
    if first:
        out_shape = out_shape + (own,)
    vmem = pl.BlockSpec(memory_space=pltpu.VMEM)
    return pl.pallas_call(
        functools.partial(update_kernel, first, last, n_leaf, n_sub),
        out_shape=out_shape,
        in_specs=[vmem] * len(args),
        out_specs=(vmem,) * len(out_shape),
        scratch_shapes=[
            pltpu.VMEM((n_sub, count, 2 * leaves, share), jnp.float32),
            pltpu.VMEM((n_sub, count, leaves, share), jnp.float32),
            pltpu.VMEM((n_sub, count, leaves, share), jnp.float32),
            pltpu.VMEM((n_sub, leaves, share), jnp.float32),
            pltpu.VMEM((n_sub, leaves, share), jnp.float32),
            pltpu.VMEM((n_leaf * n_sub, 8, LANES), jnp.float32),
            pltpu.SemaphoreType.DMA((4 * n_sub + 1,)),
            pltpu.SemaphoreType.DMA((4 * n_sub + 1,)),
        ],
        compiler_params=pltpu.CompilerParams(
            collective_id=collective_id, has_side_effects=True, vmem_limit_bytes=VMEM_LIMIT
        ),
    )(*args)


def three_parts(x):
    parts = []
    for _ in range(3):
        part = lax.reduce_precision(x, 8, 7)
        parts.append(part.astype(jnp.bfloat16))
        x = x - part
    return parts


def block_lists(offsets, counts):
    leaves, slots = offsets.shape
    total_leaves = leaves * lax.axis_size("leaf")
    anchor = jnp.arange(leaves, dtype=jnp.int32)[:, None]
    target = anchor + offsets
    slot_idx = jnp.arange(slots, dtype=jnp.int32)[None, :]
    usable = (slot_idx < counts[:, None]) & (target + lax.axis_index("leaf") * leaves < total_leaves)
    used = jnp.concatenate([jnp.ones((leaves, 1), bool), usable], axis=1).reshape(-1)
    cols = jnp.concatenate([anchor, target], axis=1).reshape(-1)
    rows = jnp.broadcast_to(anchor, (leaves, slots + 1)).reshape(-1)
    mirrors = jnp.concatenate([jnp.full((leaves, 1), 2 * leaves, jnp.int32), target], axis=1).reshape(-1)
    size = rows.shape[0]
    idx = jnp.arange(size, dtype=jnp.int32)
    used_i = used.astype(jnp.int32)
    before = jnp.sum(jnp.where(idx[None, :] < idx[:, None], used_i[None, :], 0), axis=1)
    length = -(-size // GROUP) * GROUP
    place = jnp.arange(length, dtype=jnp.int32)
    hit = (before[None, :] == place[:, None]) & used[None, :]
    any_hit = jnp.sum(hit.astype(jnp.int32), axis=1)

    def compact(values, fill):
        return jnp.sum(jnp.where(hit, values[None, :], 0), axis=1) + (1 - any_hit) * fill

    count = jnp.sum(used_i)
    return (
        compact(rows, leaves),
        compact(cols, 0),
        compact(mirrors, 2 * leaves),
        ((count + GROUP - 1) // GROUP).reshape((1,)),
    )


def body(features, occupancy, offsets, counts, right_side):
    leaves, share = right_side.shape
    n_sub = lax.axis_size("sub")
    voxels = share * n_sub
    feat = features.shape[1] * n_sub // voxels
    occ = occupancy.astype(jnp.float32)
    masked = occ * right_side
    ahead_part = shifted(features, "leaf", -1)
    ahead_masked = shifted(masked, "leaf", -1)
    owned_flat = lax.all_gather(features, "sub", axis=1, tiled=True)
    ahead_flat = lax.all_gather(ahead_part, "sub", axis=1, tiled=True)
    window = lax.all_gather(
        jnp.concatenate([masked, ahead_masked], axis=0), "sub", axis=1, tiled=True
    )
    lists = block_lists(offsets, counts)

    owned = owned_flat.reshape((leaves, feat, voxels))
    ahead = ahead_flat.reshape((leaves, feat, voxels))
    cols = jnp.concatenate([owned, ahead], axis=0)
    scale = 1.0 / (2.0 * feat)
    neg_sq = -scale * jnp.sum(jnp.square(cols.astype(jnp.float32)), axis=1)
    parts = three_parts(neg_sq)
    depth = -(-(feat + 6) // 16) * 16
    ones_c = jnp.ones((2 * leaves, 3, voxels), jnp.bfloat16)
    pad_c = jnp.zeros((2 * leaves, depth - feat - 6, voxels), jnp.bfloat16)
    col_feat = jnp.concatenate(
        [cols] + [p[:, None, :] for p in parts] + [ones_c, pad_c], axis=1
    )
    start = lax.axis_index("sub") * share
    own_rows = lax.dynamic_slice_in_dim(owned, start, share, 2)
    own_parts = [lax.dynamic_slice_in_dim(p[:leaves], start, share, 1)[:, None, :] for p in parts]
    row_feat = jnp.concatenate(
        [own_rows * jnp.bfloat16(2.0 * scale), jnp.ones((leaves, 3, share), jnp.bfloat16)]
        + own_parts
        + [jnp.zeros((leaves, depth - feat - 6, share), jnp.bfloat16)],
        axis=1,
    ).transpose((0, 2, 1))

    fwd, mir = apply_blocks(True, lists, row_feat, col_feat, masked, window)
    x, res, direction, u, win_dir, win_res, diagonal = update(
        True, False, 0, (fwd, mir, occ, right_side, window)
    )
    for it in range(1, ITERS):
        fwd, mir = apply_blocks(False, lists, row_feat, col_feat, u, win_dir)
        args = (fwd, mir, occ, direction, diagonal, x, res)
        if it == ITERS - 1:
            x, res = update(False, True, it, args)
        else:
            x, res, direction, u, win_dir, win_res = update(
                False, False, it, args + (win_dir, win_res)
            )
    return x, res


def solution(mesh):
    in_specs = (
        P(("groups", "leaf"), "sub"),
        P(("groups", "leaf"), "sub"),
        P(("groups", "leaf"), None),
        P(("groups", "leaf")),
        P(("groups", "leaf"), "sub"),
    )
    out_specs = (P(("groups", "leaf"), "sub"), P(("groups", "leaf"), "sub"))
    return jax.shard_map(body, mesh=mesh, in_specs=in_specs, out_specs=out_specs, check_vma=False)
```

time: 852 us -> 203 us (0.24); the launches traced: 839 us -> 203 us
  matrix products: 406 us -> 0 us
  blocking collectives: 169 us -> 5.43 us
  Pallas kernels: 0 us -> 113 us
  local copies, waits for them, and re-layouts: 140 us -> 35.2 us
  waiting for transfers between devices: 54.1 us -> 21.2 us
  other arithmetic: 28.2 us -> 10.2 us
  starting transfers between devices: 19.8 us -> 2.65 us
    dot_general x74 -> x0, matrix products: 406 us -> none  [the longest x3 161 us: body(): jnp.einsum('lsab,lsb->la', kernel, picked, precision=lax.Precision.HIGHEST)]
    psum x5 -> x0, blocking collectives: 151 us -> none  [the longest x3 90.9 us: residual_norm(): return lax.psum(jnp.sum(residual * residual), ('leaf', 'sub'))]
    pallas_call x0 -> x6, Pallas kernels: none -> 113 us  [the longest x3 66 us: apply_blocks(): pl.pallas_call(functools.partial(apply_kernel, with_ones), out_shape=(jax...]
    gather x134 -> x0, local copies, waits for them, and re-layouts: 83.5 us -> none  [the longest x64 36.7 us: build_leaf(): window_sq[chosen][:, None, :]]
    mul x67 -> x0, local copies, waits for them, and re-layouts: 44.9 us -> none  [the longest x64 44.7 us: build_leaf(): return jnp.exp(-distance / (2.0 * feat_width)) * weight_row[:, None, None]]
    concatenate x5 -> x7, local copies, waits for them, and re-layouts: 0.36 us -> 24.7 us  [the longest x1 21.4 us: body(): jnp.concatenate([cols] + [p[:, None, :] for p in parts] + [ones_c, pad_c]...]
    ppermute x8 -> x2, waiting for transfers between devices: 29.3 us -> 8.42 us  [shifted(): return lax.ppermute(x, axis, pairs)]
    reduce_sum x8 -> x4, other arithmetic: 24.1 us -> 3.54 us  [the longest x1 1.82 us: compact(): jnp.sum(jnp.where(hit, values[None, :], 0), axis=1) + (1 - any_hit) * fill]
  transfers between devices with their start and end apart: 13 -> 4, of which waited for: 7 -> 2; matrix products, arithmetic and copies ran while one was open for 59% -> 5% of each run, Pallas kernels for 0% -> 0%
where the time goes in v1:
time: 203 us
  Pallas kernels  113 us (56%)
  local copies, waits for them, and re-layouts  35.2 us (17%)
  waiting for transfers between devices  21.2 us (10%)
  between operations  15 us (7%)
  other arithmetic  10.2 us (5%)
  blocking collectives  5.43 us (3%)
  starting transfers between devices  2.65 us (1%)
    pallas_call x3, Pallas kernels, apply_blocks(): pl.pallas_call(functools.partial(apply_kernel, with_ones), out_shape=(jax...  66 us
    pallas_call x3, Pallas kernels, update(): pl.pallas_call(functools.partial(update_kernel, first, last, n_leaf, n_su...  47 us
    concatenate x1, local copies, waits for them, and re-layouts, body(): jnp.concatenate([cols] + [p[:, None, :] for p in parts] + [ones_c, pad_c]...  21.4 us
    all_gather x1, waiting for transfers between devices, body(): ahead_flat = lax.all_gather(ahead_part, 'sub', axis=1, tiled=True)  12 us
    ppermute x2, waiting for transfers between devices, shifted(): return lax.ppermute(x, axis, pairs)  8.42 us
    unnamed x17, local copies, waits for them, and re-layouts  6.4 us
    all_gather x1, blocking collectives, body(): lax.all_gather(jnp.concatenate([masked, ahead_masked], axis=0), 'sub', ax...  5.43 us
  transfers between devices with their start and end apart: 4, of which 2 were waited for; matrix products, arithmetic and copies ran while one was open for 5% of the time, Pallas kernels for 0%

profile of v1, /device:TPU:0, one launch (start us, length us, event | category | flops | bytes accessed | tf_op | source)
XLA Modules:
  0.0 202.6 jit_solution(5597969802730956771)
XLA Ops:
  7.2 0.7 all-gather.3.cloned.1.call-update
  7.9 1.3 collective-permute-start
  9.2 0.8 convert_multiply_fusion.u_ref
  10.0 1.3 collective-permute-start.1
  11.3 8.4 %collective-permute-done = bf16[64,2048]{1,0:T(8,128)(2,1)S(1)} collective-permute-done((bf16[64,2048]{1,0:T(8,128)(2,1)}, bf16[64,2048]{1,0:T(8,128)(2,1)S(1)}, u32[]{:S(2)}, u32[]{:S(2)}) %collective-permute-start) | collective-permute-done | bytes 262176 | tf_op jit(solution)/shard_map/ppermute | solution.py:21
  19.7 0.7 copy-done.4
  20.5 0.7 iota_add_fusion
  21.2 0.1 copy.55
  21.3 0.1 concatenate.23.clone
  21.3 0.1 broadcast_in_dim.82
  21.5 0.7 fusion.8
  22.2 0.1 copy.58
  22.3 0.1 concatenate.21.clone
  22.4 0.2 reshape.68
  22.6 0.1 copy.44
  22.7 0.1 broadcast_in_dim.80
  22.8 0.1 broadcast_in_dim.78
  23.0 0.2 select_reduce_fusion.3
  23.2 1.8 select_reduce_fusion
  25.0 0.6 convert_reduce_fusion.1
  26.3 0.8 convert_element_type.65.refs_2_
  27.2 5.4 %all_gather.11 = f32[128,256]{0,1:T(8,128)S(1)} all-gather(f32[128,64]{0,1:T(8,128)S(1)} %copy.49), channel_id=1, replica_groups=mesh['groups'=2,'leaf'=4,'sub'=4] {'sub'}, dimensions={1}, use_global_device_ids=true | all-gather | bytes 163840 | tf_op jit(solution)/shard_map/all_gather | solution.py:305
  32.6 0.1 copy.51.v_ref.refs_4_
  32.7 1.5 copy.56
  34.2 1.0 dynamic-slice_multiply_fusion
  35.2 0.1 constant_dynamic-update-slice_fusion.1
  35.3 12.0 %all-gather.5.cloned.1.call-done = bf16[64,8192]{1,0:T(8,128)(2,1)} async-done(((bf16[64,2048]{1,0:T(8,128)(2,1)}), bf16[64,8192]{1,0:T(8,128)(2,1)}) %all-gather.5.cloned.1.call-update) | async-done | bytes 1048592 | tf_op jit(solution)/shard_map/all_gather | solution.py:304
  47.3 1.5 copy.57
  48.8 0.1 constant_dynamic-update-slice_fusion
  48.9 0.9 multiply_reduce_fusion
  49.8 0.7 broadcast_multiply_fusion
  50.5 0.1 fusion.5
  50.7 0.1 fusion.7
  50.9 3.0 %concatenate.25 = bf16[64,48,64]{2,1,0:T(8,128)(2,1)S(1)} concatenate(bf16[64,32,64]{2,1,0:T(8,128)(2,1)} %dynamic-slice_multiply_fusion, bf16[64,3,64]{2,1,0:T(4,128)(2,1)S(1)} %broadcast_in_dim.84, bf16[64,1,64]{2,1,0:T(2,128)(2,1)S(1)} %copy.46, bf16[64,1,64]{2,1,0:T(2,128)(2,1)S(1)} %copy.47, bf16[64,1,64]{2,1,0:T(2,128)(2,1)S(1)} %copy.48, ...), dimensions={1} | concatenate | bytes 786432 | tf_op jit(solution)/shard_map/concatenate | solution.py:325
  53.8 1.3 copy.54.row_ref
  55.2 1.9 fusion.2
  57.1 0.8 broadcast_in_dim.89
  57.8 1.1 broadcast_in_dim.90
  58.9 21.4 %concatenate.26.col_ref = bf16[128,48,256]{2,1,0:T(8,128)(2,1)S(1)} concatenate(bf16[128,32,256]{2,1,0:T(8,128)(2,1)} %copy-done.3, bf16[128,1,256]{2,1,0:T(2,128)(2,1)} %get-tuple-element.43, bf16[128,1,256]{2,1,0:T(2,128)(2,1)} %get-tuple-element.44, bf16[128,1,256]{2,1,0:T(2,128)(2,1)S(1)} %get-tuple-element.42, bf16[128,3,256]{2,1,0:T(4,128)(2,1)} %broadcast_in_dim.89, ...), dimensions={1} | concatenate | bytes 6291456 | tf_op jit(solution)/shard_map/concatenate | solution.py:319
  80.3 1.2 copy-done
  81.5 23.9 %shard_map.68 = (f32[2,64,64]{2,1,0:T(8,128)S(1)}, f32[2,128,256]{2,1,0:T(8,128)S(1)}) custom-call(s32[896]{0:T(1024)S(1)} %get-tuple-element.49.rows_at, s32[896]{0:T(1024)S(1)} %get-tuple-element.39.cols_at, s32[896]{0:T(1024)S(1)} %get-tuple-element.48.mirror_at, s32[1]{0:T(128)} %bitcast.groups_ref, bf16[64,64,48]{2,1,0:T(8,128)(2,1)S(1)} %copy-done, ...), custom_call_target="tpu_custom_call" | custom-call | tf_op jit(solution)/shard_map/pallas_call | solution.py:70
  105.4 18.4 %shard_map.69 = (f32[64,64]{1,0:T(8,128)S(1)}, f32[64,64]{1,0:T(8,128)S(1)}, f32[64,64]{1,0:T(8,128)S(1)}, f32[64,64]{1,0:T(8,128)S(1)}, f32[128,256]{1,0:T(8,12...) custom-call(f32[2,64,64]{2,1,0:T(8,128)S(1)} %get-tuple-element.20.refs_0_, ...), custom_call_target="tpu_custom_call" | custom-call | tf_op jit(solution)/shard_map/pallas_call | solution.py:232
  123.8 21.1 %shard_map.70 = (f32[1,64,64]{2,1,0:T(8,128)S(1)}, f32[1,128,256]{2,1,0:T(8,128)S(1)}) custom-call(s32[896]{0:T(1024)S(1)} %get-tuple-element.49.rows_at, s32[896]{0:T(1024)S(1)} %get-tuple-element.39.cols_at, s32[896]{0:T(1024)S(1)} %get-tuple-element.48.mirror_at, s32[1]{0:T(128)} %bitcast.groups_ref, bf16[64,64,48]{2,1,0:T(8,128)(2,1)S(1)} %copy-done.1, ...), custom_call_target="tpu_custom_call" | custom-call | tf_op jit(solution)/shard_map/pallas_call | solution.py:70
  145.0 15.4 %shard_map.71 = (f32[64,64]{1,0:T(8,128)S(1)}, f32[64,64]{1,0:T(8,128)S(1)}, f32[64,64]{1,0:T(8,128)S(1)}, f32[64,64]{1,0:T(8,128)S(1)}, f32[128,256]{1,0:T(8,128)S(1)}, /*index=5*/f32[128,256]{1,0:T(8,128)}) custom-call(f32[1,64,64]{2,1,0:T(8,128)S(1)} %get-tuple-element.24.refs_0_, f32[1,128,256]{2,1,0:T(8,128)S(1)} %get-tuple-element.25.refs_1_, ...), custom_call_target="tpu_custom_call" | custom-call | tf_op jit(solution)/shard_map/pallas_call | solution.py:232
  160.4 21.0 %shard_map.72 = (f32[1,64,64]{2,1,0:T(8,128)S(1)}, f32[1,128,256]{2,1,0:T(8,128)S(1)}) custom-call(s32[896]{0:T(1024)S(1)} %get-tuple-element.49.rows_at, s32[896]{0:T(1024)S(1)} %get-tuple-element.39.cols_at, s32[896]{0:T(1024)S(1)} %get-tuple-element.48.mirror_at, s32[1]{0:T(128)} %bitcast.groups_ref, bf16[64,64,48]{2,1,0:T(8,128)(2,1)S(1)} %copy-done.1, ...), custom_call_target="tpu_custom_call" | custom-call | tf_op jit(solution)/shard_map/pallas_call | solution.py:70
  181.4 13.2 %shard_map.73 = (f32[64,64]{1,0:T(8,128)S(1)}, f32[64,64]{1,0:T(8,128)S(1)}) custom-call(f32[1,64,64]{2,1,0:T(8,128)S(1)} %get-tuple-element.33.refs_0_, f32[1,128,256]{2,1,0:T(8,128)S(1)} %get-tuple-element.34.refs_1_, f32[64,64]{1,0:T(8,128)S(1)} %convert_element_type.65.refs_2_, f32[64,64]{1,0:T(8,128)S(1)} %get-tuple-element.35.refs_3_, ...), custom_call_target="tpu_custom_call" | custom-call | tf_op jit(solution)/shard_map/pallas_call | solution.py:232
  194.5 0.6 copy.62
  195.2 0.6 copy.63
  (29 shorter events, 0.4 us)
Async XLA Ops:
  7.2 25.6 %all-gather.3.cloned.1.call-start = ((), (), s32[]{:S(2)}) async-start(), calls=%async_computation | async-start | bytes 1310720 | tf_op jit(solution)/shard_map/all_gather | solution.py:303
  7.9 39.4 %all-gather.5.cloned.1.call-start = ((), (), s32[]{:S(2)}) async-start(), calls=%async_computation.1 | async-start | bytes 1310720 | tf_op jit(solution)/shard_map/all_gather | solution.py:304
  7.9 11.8 %collective-permute-start = (bf16[64,2048]{1,0:T(8,128)(2,1)}, bf16[64,2048]{1,0:T(8,128)(2,1)S(1)}, u32[]{:S(2)}, u32[]{:S(2)}) collective-permute-start(bf16[64,2048]{1,0:T(8,128)(2,1)} %param.5), channel_id=1, source_target_pairs={{4,0},{8,4},{12,8},{5,1},{9,5},{13,9},{6,2},{10,6},{14,10},{7,3},{... | collective-permute-start | bytes 786440 | tf_op jit(solution)/shard_map/ppermute | solution.py:21
  10.0 17.1 %collective-permute-start.1 = (f32[64,64]{1,0:T(8,128)S(1)}, f32[64,64]{1,0:T(8,128)S(1)}, u32[]{:S(2)}, u32[]{:S(2)}) collective-permute-start(f32[64,64]{1,0:T(8,128)S(1)} %convert_multiply_fusion.u_ref), channel_id=1, source_target_pairs={{4,0},{8,4},{12,8},{5,1},{9,5},{13,9},{6,2},{10,6},{14,10},{7,3},{... | collective-permute-start | bytes 49160 | tf_op jit(solution)/shard_map/ppermute | solution.py:21
  19.7 0.7 copy-start.4
  48.9 6.3 %copy-start.3 = (bf16[128,32,256]{2,1,0:T(8,128)(2,1)}, bf16[128,32,256]{2,1,0:T(8,128)(2,1)S(1)}, u32[]{:S(2)}) copy-start(bf16[128,32,256]{2,1,0:T(8,128)(2,1)S(1)} %constant_dynamic-update-slice_fusion) | copy-start | bytes 6291460
  58.9 46.5 %copy-start.2 = (f32[64,64]{1,0:T(8,128)S(1)}, f32[64,64]{1,0:T(8,128)}, u32[]{:S(2)}) copy-start(f32[64,64]{1,0:T(8,128)} %refs_3_.1) | copy-start | bytes 49156
  80.3 1.2 copy-start
  81.5 42.3 %copy-start.1 = (bf16[64,64,48]{2,1,0:T(8,128)(2,1)S(1)}, bf16[64,64,48]{2,1,0:T(8,128)(2,1)}, u32[]{:S(2)}) copy-start(bf16[64,64,48]{2,1,0:T(8,128)(2,1)} %copy.54.row_ref) | copy-start | bytes 1179652
Sparse Core Ops, SparseCore 0:
  9.6 19.4 all-gather.2
  30.6 16.7 all-gather.4
